TPU v7x, 32 devices: a whole 2x2x4 slice. The times are simulated.
32 devices in a mesh: groups: 2 (over y), owner: 4 (over x, core), tensor: 4 (over z).
Axes of the slice: x: 2, y: 2, z: 4, core: 2. Of those that a mesh axis runs over, the one named last changes fastest.
Arguments:
- queries: bfloat16 [256, 8192], P(('groups', 'owner'), 'tensor'), parts along dimension 0, may hold values from -30 to 30
- stored_keys: bfloat16 [256, 192, 1024], P(('groups', 'owner', 'tensor')), parts along dimension 0, may hold values from -17 to 17
- stored_values: bfloat16 [256, 192, 1024], P(('groups', 'owner', 'tensor')), parts along dimension 0, may hold values from -24 to 24
- lengths: int32 [256], P(('groups', 'owner', 'tensor')), parts along dimension 0, may hold values from 2 to 192, as said below
- request_adapter: int32 [256], P(('groups', 'owner')), parts along dimension 0, may hold values from 0 to 31, as said below
- adapter_bank_row: int32 [64], P('groups'), parts along dimension 0, may hold values from 0 to 31, as said below
- output_projection_weight: bfloat16 [8192, 8192], P('tensor'), may hold values from -0.09375 to 0.09375
- adapter_down_weight: float32 [64, 8192, 64], P(('groups', 'owner'), 'tensor'), parts along dimension 0, may hold values from -0.0625 to 0.0625
- adapter_up_weight: float32 [64, 64, 8192], P(('groups', 'owner'), None, 'tensor'), parts along dimension 0, may hold values from -0.75 to 0.75
Outputs:
- layer_output: bfloat16 [256, 8192], P(('groups', 'owner'), 'tensor'), parts along dimension 0
There are 2 independent parts, one for each index of `groups`. A program takes and returns all parts, laid end to end along the dimension named above; an argument that names none is the same for every part. Nothing has to cross between parts.
Inputs may be any that keep to these rules, and one draw needn't show every extreme that they name: `lengths`: one request of the group has exactly 192 valid positions. The 32 requests of one index of owner are rows o * 32 to (o + 1) * 32 - 1. Among them at most 16 have a bank row adapter_bank_row[request_adapter[r]] with the same quotient by 8; for one quotient, the same for all subgroups, exactly 16 do in every subgroup. `adapter_bank_row`: A permutation of the adapters.
All inputs are finite; a program needn't handle non-finite values.
Results may differ from a plain program's by a relative error of at most 0.0055.
Values may be sent and summed in bfloat16 or wider, within the bound.
A program may use at most 192 MiB of HBM per device.

v0:
```python
import math

import jax
import jax.numpy as jnp
from jax import lax
from jax.sharding import PartitionSpec as P

HQ = 64
KVH = 8
HEAD = 128


def attend_rows(query_rows, stored_keys, stored_values, lengths):
    count = query_rows.shape[0]
    positions = stored_keys.shape[1]
    group_size = HQ // KVH
    query_heads = query_rows.reshape(count, KVH, group_size, HEAD)
    key_heads = stored_keys.reshape(count, positions, KVH, HEAD)
    value_heads = stored_values.reshape(count, positions, KVH, HEAD)
    scores = jnp.einsum(
        "rgjd,rpgd->rgjp", query_heads, key_heads, preferred_element_type=jnp.float32
    ) * (1.0 / math.sqrt(HEAD))
    valid = (jnp.arange(positions)[None, :] < lengths[:, None])[:, None, None, :]
    scores = jnp.where(valid, scores, -1e30)
    highest = jnp.max(scores, axis=-1, keepdims=True)
    expo = jnp.where(valid, jnp.exp(scores - highest), 0.0)
    total = jnp.sum(expo, axis=-1, keepdims=True)
    weights = expo.astype(jnp.bfloat16)
    mixed = jnp.einsum("rgjp,rpgd->rgjd", weights, value_heads, preferred_element_type=jnp.float32)
    return (mixed / total).astype(jnp.bfloat16).reshape(count, HQ * HEAD)


def local(
    queries,
    stored_keys,
    stored_values,
    lengths,
    request_adapter,
    adapter_bank_row,
    output_projection_weight,
    adapter_down_weight,
    adapter_up_weight,
):
    highest_precision = lax.Precision.HIGHEST
    query_rows = lax.all_to_all(queries, "tensor", split_axis=0, concat_axis=1, tiled=True)
    attended = attend_rows(query_rows, stored_keys, stored_values, lengths)
    head_rows = lax.all_to_all(attended, "tensor", split_axis=1, concat_axis=0, tiled=True)
    partial_value = jnp.dot(head_rows, output_projection_weight, preferred_element_type=jnp.float32)
    base = lax.psum_scatter(partial_value, "tensor", scatter_dimension=1, tiled=True)
    adapter_count = adapter_bank_row.shape[0]
    matches = request_adapter[:, None] == jnp.arange(adapter_count, dtype=jnp.int32)[None, :]
    bank_rows = jnp.sum(jnp.where(matches, adapter_bank_row[None, :], 0), axis=1)
    head_values = head_rows.astype(jnp.float32)
    output_share = lax.all_gather(adapter_down_weight, "owner", axis=0, tiled=True)
    span = output_share.shape[0]
    selector = (bank_rows[:, None] == jnp.arange(span, dtype=jnp.int32)[None, :]).astype(
        jnp.float32
    )
    projected = jnp.einsum("rk,akj->raj", head_values, output_share, precision=highest_precision)
    down_part = jnp.einsum("ra,raj->rj", selector, projected, precision=highest_precision)
    down_whole = lax.psum(down_part, "tensor")
    output_share = lax.all_gather(adapter_up_weight, "owner", axis=0, tiled=True)
    span = output_share.shape[0]
    selector = (bank_rows[:, None] == jnp.arange(span, dtype=jnp.int32)[None, :]).astype(
        jnp.float32
    )
    lifted_all = jnp.einsum("rj,ajc->rac", down_whole, output_share, precision=highest_precision)
    adapted = jnp.einsum("ra,rac->rc", selector, lifted_all, precision=highest_precision)
    return (base + adapted).astype(jnp.bfloat16)


def solution(mesh):
    return jax.shard_map(
        local,
        mesh=mesh,
        in_specs=(
            P(("groups", "owner"), "tensor"),
            P(("groups", "owner", "tensor"), None, None),
            P(("groups", "owner", "tensor"), None, None),
            P(("groups", "owner", "tensor")),
            P(("groups", "owner")),
            P("groups"),
            P("tensor", None),
            P(("groups", "owner"), "tensor", None),
            P(("groups", "owner"), None, "tensor"),
        ),
        out_specs=P(("groups", "owner"), "tensor"),
        check_vma=False,
    )
```

profile of v0, /device:TPU:0, one launch (start us, length us, event | category | flops | bytes accessed | tf_op | source)
XLA Modules:
  0.0 253.9 jit_solution(8640906530792551114)
XLA Ops:
  7.4 0.0 copy-start
  7.4 0.0 copy-start.4
  7.4 0.0 copy-start.3
  7.4 0.0 copy-start.2
  7.4 0.0 all-gather.3.cloned.1.call-start
  7.4 0.7 all-gather.3.cloned.1.call-update
  8.1 0.0 all-gather.5.cloned.1.call-start
  8.2 0.7 all-gather.5.cloned.1.call-update
  8.9 6.3 %all-to-all-start = ((bf16[4,8,2048]{2,1,0:T(8,128)(2,1)}), bf16[4,8,2048]{2,1,0:T(8,128)(2,1)S(1)}, u32[]{:S(2)}, u32[]{:S(2)}) async-start(bf16[4,8,2048]{2,1,0:T(8,128)(2,1)} %bitcast), calls=%async_computation | async-start | bytes 262144 | tf_op jit(solution)/shard_map/all_to_all | solution.py:45
  15.2 0.0 copy-done.4
  15.2 0.0 copy-done.3
  15.2 0.2 select_reduce_fusion
  15.4 0.0 copy-done.2
  15.4 0.1 iota_compare_fusion.2
  15.5 5.8 %all-to-all-done = bf16[4,8,2048]{2,1,0:T(8,128)(2,1)S(1)} async-done(((bf16[4,8,2048]{2,1,0:T(8,128)(2,1)}), bf16[4,8,2048]{2,1,0:T(8,128)(2,1)S(1)}, u32[]{:S(2)}, u32[]{:S(2)}) %all-to-all-start) | async-done | bytes 131104 | tf_op jit(solution)/shard_map/all_to_all | solution.py:45
  21.3 0.1 copy.21
  21.4 0.1 reshape.40
  21.5 0.0 copy-done
  21.5 2.5 fusion.37
  24.0 3.5 %fusion.21 = bf16[8,8,8,128]{3,2,1,0:T(8,128)(2,1)S(1)} fusion(bf16[8,8,8,192]{3,2,1,0:T(8,128)(2,1)} %get-tuple-element.6, f32[8,8,8]{2,1,0:T(8,128)S(1)} %get-tuple-element.5, bf16[8,192,1024]{2,1,0:T(8,128)(2,1)} %param.11), kind=kOutput, calls=%fused_computation.15 | convolution fusion | flops 25296896 | bytes 3475456 | tf_op jit(solution)/shard_map/rgjp,rpgd->rgjd/dot_general | solution.py:29
  27.5 0.7 copy.24
  28.3 3.3 %all-to-all-start.1 = ((bf16[8,4,2048]{2,0,1:T(8,128)(2,1)}), bf16[8,4,2048]{2,0,1:T(8,128)(2,1)S(1)}, u32[]{:S(2)}, u32[]{:S(2)}) async-start(bf16[8,4,2048]{2,0,1:T(8,128)(2,1)} %copy.24), calls=%async_computation.1 | async-start | bytes 262144 | tf_op jit(solution)/shard_map/all_to_all | solution.py:47
  31.6 0.0 reduce-scatter.2.cloned.1.call-start
  31.7 0.1 fusion.36
  31.7 5.8 %all-to-all-done.1 = bf16[8,4,2048]{2,0,1:T(8,128)(2,1)S(1)} async-done(((bf16[8,4,2048]{2,0,1:T(8,128)(2,1)}), bf16[8,4,2048]{2,0,1:T(8,128)(2,1)S(1)}, u32[]{:S(2)}, u32[]{:S(2)}) %all-to-all-start.1) | async-done | bytes 131104 | tf_op jit(solution)/shard_map/all_to_all | solution.py:47
  37.5 14.7 %fusion.30 = f32[32,8192]{1,0:T(8,128)} fusion(bf16[2048,8192]{1,0:T(8,128)(2,1)} %param.15, bf16[8,4,2048]{2,0,1:T(8,128)(2,1)S(1)} %all-to-all-done.1), kind=kOutput, calls=%fused_computation.23 | convolution fusion | flops 1073741824 | bytes 34734080 | tf_op jit(solution)/shard_map/dot_general | solution.py:48
  52.2 0.0 reduce-scatter.2.cloned.1.call-update
  52.2 66.3 %all-gather.3.cloned.1.call-done = f32[32,2048,64]{1,2,0:T(8,128)} async-done(((f32[8,2048,64]{1,2,0:T(8,128)}), f32[32,2048,64]{1,2,0:T(8,128)}) %all-gather.3.cloned.1.call-update) | async-done | bytes 16777232 | tf_op jit(solution)/shard_map/all_gather | solution.py:54
  118.5 14.8 %fusion.28 = f32[32,32,64]{2,0,1:T(8,128)S(1)} fusion(f32[32,2048,64]{1,2,0:T(8,128)} %all-gather.3.cloned.1.call-done, bf16[8,4,2048]{2,0,1:T(8,128)(2,1)S(1)} %all-to-all-done.1), kind=kOutput, calls=%fused_computation.21 | convolution fusion | flops 1610612736 | bytes 17170432 | tf_op jit(solution)/shard_map/rk,akj->raj/dot_general | solution.py:59
  133.3 0.6 fusion.24
  133.9 18.7 %psum.7 = f32[32,64]{1,0:T(8,128)S(1)} all-reduce(f32[32,64]{1,0:T(8,128)S(1)} %bitcast.55), channel_id=1, replica_groups=mesh['groups'=2,'owner'=4,'tensor'=4] {'tensor'}, use_global_device_ids=true, to_apply=%region_4.5 | all-reduce | flops 2048 | bytes 16384 | tf_op jit(solution)/shard_map/psum | solution.py:61
  152.7 73.4 %all-gather.5.cloned.1.call-done = f32[32,64,2048]{2,1,0:T(8,128)} async-done(((f32[8,64,2048]{2,1,0:T(8,128)}), f32[32,64,2048]{2,1,0:T(8,128)}) %all-gather.5.cloned.1.call-update) | async-done | bytes 16777232 | tf_op jit(solution)/shard_map/all_gather | solution.py:62
  226.1 0.0 copy-start.1
  226.1 11.0 %fusion.34 = f32[32,32,2048]{2,0,1:T(8,128)S(1)} fusion(f32[32,64,2048]{2,1,0:T(8,128)} %all-gather.5.cloned.1.call-done, f32[32,64]{1,0:T(8,128)S(1)} %psum.7), kind=kOutput, calls=%fused_computation.27 | convolution fusion | flops 1610612736 | bytes 25174016 | tf_op jit(solution)/shard_map/rj,ajc->rac/dot_general | solution.py:67
  237.1 7.6 %fusion.1 = f32[32,1,2048]{2,1,0:T(1,128)S(1)} fusion(f32[32,32,2048]{2,0,1:T(8,128)S(1)} %fusion.34, pred[32,32,1]{1,0,2:T(32,128)(4,1)S(1)} %fusion.36), kind=kOutput, calls=%fused_computation.1 | convolution fusion | flops 25165824 | bytes 8651776 | tf_op jit(solution)/shard_map/ra,rac->rc/dot_general | solution.py:68
  244.7 0.0 reduce-scatter.2.cloned.1.call-done
  244.7 1.7 fusion.26
  246.4 0.0 copy-done.1
  (1 shorter events, 0.0 us)
Async XLA Ops:
  7.4 14.1 %copy-start = (bf16[8,192,1024]{2,1,0:T(8,128)(2,1)S(1)}, bf16[8,192,1024]{2,1,0:T(8,128)(2,1)}, u32[]{:S(2)}) copy-start(bf16[8,192,1024]{2,1,0:T(8,128)(2,1)} %param.10) | copy-start | bytes 9437188
  7.4 7.8 %copy-start.4 = (s32[32]{0:T(128)S(1)}, s32[32]{0:T(128)}, u32[]{:S(2)}) copy-start(s32[32]{0:T(128)} %param.13) | copy-start | bytes 388
  7.4 7.8 %copy-start.3 = (s32[32]{0:T(128)S(1)}, s32[32]{0:T(128)}, u32[]{:S(2)}) copy-start(s32[32]{0:T(128)} %param.14) | copy-start | bytes 388
  7.4 8.0 %copy-start.2 = (s32[8]{0:T(128)S(1)}, s32[8]{0:T(128)}, u32[]{:S(2)}) copy-start(s32[8]{0:T(128)} %param.12) | copy-start | bytes 100
  7.4 111.1 %all-gather.3.cloned.1.call-start = ((), (), s32[]{:S(2)}) async-start(), calls=%async_computation.4 | async-start | bytes 20971520 | tf_op jit(solution)/shard_map/all_gather | solution.py:54
  8.1 218.0 %all-gather.5.cloned.1.call-start = ((), (), s32[]{:S(2)}) async-start(), calls=%async_computation.5 | async-start | bytes 20971520 | tf_op jit(solution)/shard_map/all_gather | solution.py:62
  8.9 12.4 %all-to-all-start = ((bf16[4,8,2048]{2,1,0:T(8,128)(2,1)}), bf16[4,8,2048]{2,1,0:T(8,128)(2,1)S(1)}, u32[]{:S(2)}, u32[]{:S(2)}) async-start(bf16[4,8,2048]{2,1,0:T(8,128)(2,1)} %bitcast), calls=%async_computation | async-start | bytes 262144 | tf_op jit(solution)/shard_map/all_to_all | solution.py:45
  28.3 9.2 %all-to-all-start.1 = ((bf16[8,4,2048]{2,0,1:T(8,128)(2,1)}), bf16[8,4,2048]{2,0,1:T(8,128)(2,1)S(1)}, u32[]{:S(2)}, u32[]{:S(2)}) async-start(bf16[8,4,2048]{2,0,1:T(8,128)(2,1)} %copy.24), calls=%async_computation.1 | async-start | bytes 262144 | tf_op jit(solution)/shard_map/all_to_all | solution.py:47
  31.6 213.1 %reduce-scatter.2.cloned.1.call-start = ((), (), s32[]{:S(2)}) async-start(), calls=%async_computation.3 | async-start | bytes 1310720 | tf_op jit(solution)/shard_map/reduce_scatter | solution.py:49
  226.1 20.3 %copy-start.1 = (bf16[8,192,1024]{2,1,0:T(8,128)(2,1)S(1)}, bf16[8,192,1024]{2,1,0:T(8,128)(2,1)}, u32[]{:S(2)}) copy-start(bf16[8,192,1024]{2,1,0:T(8,128)(2,1)} %param.10) | copy-start | bytes 9437188
Sparse Core Ops, SparseCore 0:
  9.8 108.6 all-gather.2
  120.1 105.9 all-gather.4
Sparse Core Ops, SparseCore 1:
  52.3 26.3 reduce-scatter.1
where the time goes:
time: 254 us
  waiting for transfers between devices  153 us (60%)
  matrix products  54.7 us (22%)
  blocking collectives  18.7 us (7%)
  between operations  14.9 us (6%)
  starting transfers between devices  9.77 us (4%)
    all_gather x1, waiting for transfers between devices, local(): lax.all_gather(adapter_up_weight, 'owner', axis=0, tiled=True)  73.4 us
    all_gather x1, waiting for transfers between devices, local(): lax.all_gather(adapter_down_weight, 'owner', axis=0, tiled=True)  66.3 us
    psum x1, blocking collectives, local(): down_whole = lax.psum(down_part, 'tensor')  18.7 us
    dot_general x1, matrix products, local(): jnp.einsum('rk,akj->raj', head_values, output_share, precision=highest_pr...  14.8 us
    dot_general x1, matrix products, local(): jnp.dot(head_rows, output_projection_weight, preferred_element_type=jnp.f...  14.7 us
    dot_general x1, matrix products, local(): jnp.einsum('rj,ajc->rac', down_whole, output_share, precision=highest_pre...  11 us
    dot_general x1, matrix products, local(): jnp.einsum('ra,rac->rc', selector, lifted_all, precision=highest_precision)  7.64 us
    all_to_all x1, starting transfers between devices, local(): lax.all_to_all(queries, 'tensor', split_axis=0, concat_axis=1, tiled=True)  6.33 us
  transfers between devices with their start and end apart: 5, of which 4 were waited for; matrix products, arithmetic and copies ran while one was open for 22% of the time, Pallas kernels for 0%

commit v1 on v0

v1 whole, which is shorter than its diff:
```python
import functools
import math

import jax
import jax.numpy as jnp
from jax import lax
from jax.experimental import pallas as pl
from jax.experimental.pallas import tpu as pltpu
from jax.sharding import PartitionSpec as P

HQ = 64
KVH = 8
HEAD = 128
F32 = jnp.float32
BF16 = jnp.bfloat16
NT = (((1,), (1,)), ((), ()))


def kernel(
    T, O, CAP, TN,
    q_ref, len_ref, ra_ref, abr_ref, k_hbm, v_hbm, w_hbm, d_hbm, u_hbm,
    out_ref,
    kv_k, kv_v, w_v, d_f, u_f, d_b, u_b,
    qs, qr, qf, attf, atts, attr, xf, xb,
    sel_t, disp, grecv, ds, dr, rs, rr, ps, pr, own,
    lk, lv, lw, ld, lu,
    s_q, r_q, s_a, r_a, s_g, r_g, s_d, r_d, s_r, r_r, s_p, r_p,
):
    me = lax.axis_index("tensor")
    mo = lax.axis_index("owner")
    R, KB = q_ref.shape
    CB = out_ref.shape[1]
    NR = k_hbm.shape[0]
    POS = k_hbm.shape[1]
    HT = HQ // T
    AO, RANK = u_hbm.shape[0], u_hbm.shape[1]
    OC = O * CAP
    far = [(T // 2 + i) % T for i in range(T) if (T // 2 + i) % T != 0]

    loads_k, loads_v = [], []
    for r in range(NR):
        loads_k.append(pltpu.make_async_copy(k_hbm.at[r], kv_k.at[r], lk.at[r]))
        loads_v.append(pltpu.make_async_copy(v_hbm.at[r], kv_v.at[r], lv.at[r]))
        loads_k[r].start()
        loads_v[r].start()
    load_d = pltpu.make_async_copy(d_hbm, d_f, ld)
    load_u = pltpu.make_async_copy(u_hbm, u_f, lu)
    load_d.start()
    load_u.start()
    loads_w = {}
    for k in far + [0]:
        to = lax.rem(me + k, T)
        loads_w[k] = pltpu.make_async_copy(
            w_hbm.at[:, pl.ds(pl.multiple_of(to * CB, CB), CB)], w_v.at[k], lw.at[k]
        )
        loads_w[k].start()

    barrier = pltpu.get_barrier_semaphore()
    for k in range(1, T):
        pl.semaphore_signal(barrier, inc=1, device_id={"tensor": lax.rem(me + k, T)})
    for k in range(1, O):
        pl.semaphore_signal(barrier, inc=1, device_id={"owner": lax.rem(mo + k, O)})

    for t in range(T):
        rows = q_ref[t * NR:(t + 1) * NR, :].astype(F32)
        qs[t] = jnp.concatenate(
            [rows[:, h * HEAD:(h + 1) * HEAD] for h in range(HT)], axis=0
        ).astype(BF16)
    pl.semaphore_wait(barrier, T + O - 2)

    def to_tensor(k, src, dst, ss, rs_):
        c = pltpu.make_async_remote_copy(
            src_ref=src, dst_ref=dst, send_sem=ss.at[k], recv_sem=rs_.at[k],
            device_id={"tensor": lax.rem(me + k, T)},
        )
        c.start()
        return c

    def to_owner(k, target, src, dst, ss, rs_):
        c = pltpu.make_async_remote_copy(
            src_ref=src, dst_ref=dst, send_sem=ss.at[k], recv_sem=rs_.at[k],
            device_id={"owner": target},
        )
        c.start()
        return c

    sent = []
    cq = [to_tensor(k, qs.at[lax.rem(me + k, T)], qr.at[me], s_q, r_q) for k in far]
    sent += cq
    qr[me] = qs[me]

    A = abr_ref.shape[1]
    ia = lax.broadcasted_iota(jnp.int32, (A, A), 0)
    la = lax.broadcasted_iota(jnp.int32, (A, A), 1)
    abr_col = jnp.sum(jnp.where(ia == la, abr_ref[...], 0), axis=1, keepdims=True)
    hits = lax.broadcasted_iota(jnp.int32, (A, R), 0) == ra_ref[...]
    bank = jnp.sum(jnp.where(hits, abr_col, 0), axis=0, keepdims=True)
    who = bank // AO
    inner = bank - who * AO
    OP = max(8, O)
    eq = (lax.broadcasted_iota(jnp.int32, (OP, R), 0) == who).astype(F32)
    ir = lax.broadcasted_iota(jnp.int32, (R, R), 0)
    lr = lax.broadcasted_iota(jnp.int32, (R, R), 1)
    before = jnp.dot(
        eq.astype(BF16), (ir < lr).astype(F32).astype(BF16), preferred_element_type=F32
    )
    rank = jnp.sum(eq * before, axis=0, keepdims=True).astype(jnp.int32)
    place = who * CAP + rank
    sel = (lax.broadcasted_iota(jnp.int32, (OC, R), 0) == place).astype(F32).astype(BF16)
    place_col = jnp.sum(jnp.where(ir == lr, place, 0), axis=1, keepdims=True)
    sel_t[...] = (
        (lax.broadcasted_iota(jnp.int32, (R, OC), 1) == place_col).astype(F32).astype(BF16)
    )
    inner_t = (lax.broadcasted_iota(jnp.int32, (128, R), 0) == inner).astype(F32).astype(BF16)
    marks = lax.dot_general(sel, inner_t, NT, preferred_element_type=F32).astype(BF16)
    for o in range(O):
        disp[o, :, KB:] = marks[o * CAP:(o + 1) * CAP, :]

    for c in cq:
        c.wait_recv()
    for t in range(T):
        qf[t * HT * NR:(t + 1) * HT * NR, :] = qr[t].astype(F32)

    G = HQ // KVH
    head_of = lax.broadcasted_iota(jnp.int32, (HQ, KVH * HEAD), 0) // G
    lane_of = lax.broadcasted_iota(jnp.int32, (HQ, KVH * HEAD), 1) // HEAD
    diagonal = head_of == lane_of
    pos = lax.broadcasted_iota(jnp.int32, (HQ, POS), 1)
    for r in range(NR):
        q_r = qf[pl.ds(r, HQ, stride=NR), :]
        wide = jnp.where(diagonal, jnp.concatenate([q_r] * KVH, axis=1), 0.0).astype(BF16)
        loads_k[r].wait()
        scores = lax.dot_general(wide, kv_k[r], NT, preferred_element_type=F32)
        scores = scores * (1.0 / math.sqrt(HEAD))
        valid = pos < len_ref[r]
        scores = jnp.where(valid, scores, -1e30)
        highest = jnp.max(scores, axis=1, keepdims=True)
        expo = jnp.where(valid, jnp.exp(scores - highest), 0.0)
        total = jnp.sum(expo, axis=1, keepdims=True)
        loads_v[r].wait()
        mixed = jnp.dot(expo.astype(BF16), kv_v[r], preferred_element_type=F32)
        mixed = jnp.concatenate(
            [mixed[g * G:(g + 1) * G, g * HEAD:(g + 1) * HEAD] for g in range(KVH)], axis=0
        )
        attf[pl.ds(r, HQ, stride=NR), :] = mixed / total
    for t in range(T):
        atts[t] = attf[t * HT * NR:(t + 1) * HT * NR, :].astype(BF16)
    ca = [to_tensor(k, atts.at[lax.rem(me + k, T)], attr.at[me], s_a, r_a) for k in far]
    sent += ca
    attr[me] = atts[me]

    load_d.wait()
    load_u.wait()

    @pl.loop(0, AO)
    def _(a):
        rows = pl.ds(pl.multiple_of(a * RANK, RANK), RANK)
        d_b[rows, :] = d_f[a].astype(BF16)
        u_b[rows, :] = u_f[a].astype(BF16)

    for c in ca:
        c.wait_recv()
    for t in range(T):
        got = attr[t].astype(F32)
        for h in range(HT):
            xf[t * NR:(t + 1) * NR, h * HEAD:(h + 1) * HEAD] = got[h * NR:(h + 1) * NR, :]
    xb[...] = xf[...].astype(BF16)

    disp_rows = jnp.dot(sel, xb[...], preferred_element_type=F32).astype(BF16)
    for o in range(O):
        disp[o, :, :KB] = disp_rows[o * CAP:(o + 1) * CAP, :]
    cg = []
    for k in range(1, O):
        o = lax.rem(mo + k, O)
        cg.append(to_owner(k, o, disp.at[o], grecv.at[mo], s_g, r_g))
    sent += cg
    grecv[mo] = disp[mo]

    def project(k):
        loads_w[k].wait()

        @pl.loop(0, CB // TN)
        def _(j):
            cols = pl.ds(pl.multiple_of(j * TN, TN), TN)
            part = jnp.dot(xb[...], w_v[k, :, cols], preferred_element_type=F32)
            if k:
                ps[k, :, cols] = part.astype(BF16)
            else:
                own[:, cols] = part

    cp = []

    def project_and_send(k):
        project(k)
        cp.append(to_tensor(k, ps.at[k], pr.at[me], s_p, r_p))

    half = max(1, len(far) // 3)
    for k in far[:half]:
        project_and_send(k)

    for c in cg:
        c.wait_recv()
    rows_in = grecv[...].reshape(OC, KB + 128)
    ej = lax.broadcasted_iota(jnp.int32, (128, AO * RANK), 0)
    el = lax.broadcasted_iota(jnp.int32, (128, AO * RANK), 1) // RANK
    spread = (ej == el).astype(F32).astype(BF16)
    mask = jnp.dot(rows_in[:, KB:], spread, preferred_element_type=F32)
    every = lax.dot_general(rows_in[:, :KB], d_b[...], NT, preferred_element_type=F32) * mask
    lanes = every[:, :128]
    for i in range(1, AO * RANK // 128):
        lanes = lanes + every[:, i * 128:(i + 1) * 128]
    down = lanes[:, :RANK] + lanes[:, RANK:]
    ds[...] = jnp.concatenate([down[:OC // 2], down[OC // 2:]], axis=1)
    cd = [to_tensor(k, ds, dr.at[me], s_d, r_d) for k in far]
    sent += cd

    for k in far[half:]:
        project_and_send(k)
    sent += cp

    for c in cd:
        c.wait_recv()
    total_down = ds[...]
    for k in range(1, T):
        total_down = total_down + dr[lax.rem(me + k, T)]
    down = jnp.concatenate([total_down[:, :RANK], total_down[:, RANK:]], axis=0)
    twice = jnp.concatenate([down, down], axis=1)
    lifted_in = (jnp.concatenate([twice] * (AO * RANK // 128), axis=1) * mask).astype(BF16)
    lifted = jnp.dot(lifted_in, u_b[...], preferred_element_type=F32).astype(BF16)
    for o in range(O):
        rs[o] = lifted[o * CAP:(o + 1) * CAP, :]
    cr = []
    for k in range(1, O):
        o = lax.rem(mo + k, O)
        cr.append(to_owner(k, o, rs.at[o], rr.at[mo], s_r, r_r))
    sent += cr
    rr[mo] = rs[mo]

    project(0)
    for c in cp:
        c.wait_recv()
    for c in cr:
        c.wait_recv()
    step = min(512, CB)
    for j in range(CB // step):
        cols = slice(j * step, (j + 1) * step)
        whole = jnp.dot(
            sel_t[...], rr[:, :, cols].reshape(OC, step), preferred_element_type=F32
        )
        base = own[:, cols]
        for k in range(1, T):
            base = base + pr[lax.rem(me + k, T), :, cols].astype(F32)
        out_ref[:, cols] = (base + whole).astype(BF16)
    for c in sent:
        c.wait_send()


def local(mesh, q, k, v, lengths, ra, abr, w, d, u):
    T, O = mesh.shape["tensor"], mesh.shape["owner"]
    R, KB = q.shape
    NR, POS, KW = k.shape
    AO, RANK, CB = u.shape
    CAP = 2 * R // O
    OC = O * CAP
    HT = HQ // T
    TN = min(512, CB)
    vm = pltpu.VMEM
    dma = pltpu.SemaphoreType.DMA
    scratch = [
        vm((NR, POS, KW), BF16), vm((NR, POS, KW), BF16),
        vm((T, KB, CB), BF16),
        vm((AO, RANK, KB), F32), vm((AO, RANK, CB), F32),
        vm((AO * RANK, KB), BF16), vm((AO * RANK, CB), BF16),
        vm((T, HT * NR, HEAD), BF16), vm((T, HT * NR, HEAD), BF16), vm((HQ * NR, HEAD), F32),
        vm((HQ * NR, HEAD), F32), vm((T, HT * NR, HEAD), BF16), vm((T, HT * NR, HEAD), BF16),
        vm((R, KB), F32), vm((R, KB), BF16),
        vm((R, OC), BF16), vm((O, CAP, KB + 128), BF16), vm((O, CAP, KB + 128), BF16),
        vm((OC // 2, 2 * RANK), F32), vm((T, OC // 2, 2 * RANK), F32),
        vm((O, CAP, CB), BF16), vm((O, CAP, CB), BF16),
        vm((T, R, CB), BF16), vm((T, R, CB), BF16), vm((R, CB), F32),
        dma((NR,)), dma((NR,)), dma((T,)), dma(()), dma(()),
        dma((T,)), dma((T,)), dma((T,)), dma((T,)), dma((O,)), dma((O,)),
        dma((T,)), dma((T,)), dma((O,)), dma((O,)), dma((T,)), dma((T,)),
    ]
    any_spec = pl.BlockSpec(memory_space=pl.ANY)
    vmem_spec = pl.BlockSpec(memory_space=pltpu.VMEM)
    smem_spec = pl.BlockSpec(memory_space=pltpu.SMEM)
    return pl.pallas_call(
        functools.partial(kernel, T, O, CAP, TN),
        out_shape=jax.ShapeDtypeStruct((R, CB), BF16),
        in_specs=[vmem_spec, smem_spec, vmem_spec, vmem_spec] + [any_spec] * 5,
        out_specs=vmem_spec,
        scratch_shapes=scratch,
        compiler_params=pltpu.CompilerParams(
            collective_id=0, has_side_effects=True, vmem_limit_bytes=60 * 2**20
        ),
        name="attend_project_adapt",
    )(q, lengths, ra.reshape(1, -1), abr.reshape(1, -1), k, v, w, jnp.swapaxes(d, 1, 2), u)


def solution(mesh):
    return jax.shard_map(
        functools.partial(local, mesh),
        mesh=mesh,
        in_specs=(
            P(("groups", "owner"), "tensor"),
            P(("groups", "owner", "tensor"), None, None),
            P(("groups", "owner", "tensor"), None, None),
            P(("groups", "owner", "tensor")),
            P(("groups", "owner")),
            P("groups"),
            P("tensor", None),
            P(("groups", "owner"), "tensor", None),
            P(("groups", "owner"), None, "tensor"),
        ),
        out_specs=P(("groups", "owner"), "tensor"),
        check_vma=False,
    )
```

time: 254 us -> 38.9 us (0.15)
  waiting for transfers between devices: 153 us -> 0 us
  matrix products: 54.7 us -> 0 us
  Pallas kernels: 0 us -> 37.1 us
  blocking collectives: 18.7 us -> 0 us
  between operations: 14.9 us -> 0.01 us
  starting transfers between devices: 9.77 us -> 0 us
    all_gather x2 -> x0, waiting for transfers between devices: 140 us -> none  [the longest x1 73.4 us: local(): lax.all_gather(adapter_up_weight, 'owner', axis=0, tiled=True)]
    dot_general x6 -> x0, matrix products: 52.2 us -> none  [the longest x1 14.8 us: local(): jnp.einsum('rk,akj->raj', head_values, output_share, precision=highest_pr...]
    pallas_call x0 -> x1, Pallas kernels: none -> 37.1 us  [local(): pl.pallas_call(functools.partial(kernel, T, O, CAP, TN), out_shape=jax.Sh...]
    psum x1 -> x0, blocking collectives: 18.7 us -> none  [local(): down_whole = lax.psum(down_part, 'tensor')]
    all_to_all x2 -> x0, waiting for transfers between devices: 11.6 us -> none  [the longest x1 5.81 us: local(): lax.all_to_all(queries, 'tensor', split_axis=0, concat_axis=1, tiled=True)]
    all_to_all x2 -> x0, starting transfers between devices: 9.66 us -> none  [the longest x1 6.33 us: local(): lax.all_to_all(queries, 'tensor', split_axis=0, concat_axis=1, tiled=True)]
  transfers between devices with their start and end apart: 5 -> 0, of which waited for: 4 -> 0; matrix products, arithmetic and copies ran while one was open for 22% -> 0% of each run, Pallas kernels for 0% -> 0%
where the time goes in v1:
time: 38.9 us; the launch traced here: 38.7 us
  Pallas kernels  37.1 us (95%)
  local copies, waits for them, and re-layouts  1.57 us (4%)
    pallas_call x1, Pallas kernels, local(): pl.pallas_call(functools.partial(kernel, T, O, CAP, TN), out_shape=jax.Sh...  37.1 us
    unnamed x1, local copies, waits for them, and re-layouts  1.57 us

profile of v1, /device:TPU:0, one launch (start us, length us, event | category | flops | bytes accessed | tf_op | source)
XLA Modules:
  0.0 38.7 jit_solution(6234499849310287713)
XLA Ops:
  0.0 37.1 %attend_project_adapt.1 = bf16[32,2048]{1,0:T(8,128)(2,1)} custom-call(bf16[32,2048]{1,0:T(8,128)(2,1)} %q_ref.1, s32[8]{0:T(128)} %len_ref.1, s32[1,32]{1,0:T(1,128)} %bitcast.4, s32[1,32]{1,0:T(1,128)} %bitcast.5, bf16[8,192,1024]{2,1,0:T(8,128)(2,1)} %k_hbm.1, bf16[8,192,1024]{2,1,0:T(8,128)(2,1)} %v_hbm.1, bf16[2048,8192]{1,0:T(8,128)(2,1)} %w_hbm.1, ...), custom_call_target="tpu_custom_call" | custom-call | tf_op jit(solution)/shard_map/attend_project_adapt/pallas_call | solution.py:288
  37.1 1.6 %copy.11 = bf16[32,2048]{1,0:T(8,128)(2,1)} copy(bf16[32,2048]{1,0:T(8,128)(2,1)} %attend_project_adapt.1) | data formatting | bytes 262144

commit v2 on v1

--- a/solution.py
+++ b/solution.py
@@ -22,7 +22,7 @@
     out_ref,
     kv_k, kv_v, w_v, d_f, u_f, d_b, u_b,
     qs, qr, qf, attf, atts, attr, xf, xb,
-    sel_t, disp, grecv, ds, dr, rs, rr, ps, pr, own,
+    sel_t, disp, grecv, ds, dr, rs, rr, ps, pr, own, passing,
     lk, lv, lw, ld, lu,
     s_q, r_q, s_a, r_a, s_g, r_g, s_d, r_d, s_r, r_r, s_p, r_p,
 ):
@@ -47,13 +47,18 @@
     load_u = pltpu.make_async_copy(u_hbm, u_f, lu)
     load_d.start()
     load_u.start()
-    loads_w = {}
-    for k in far + [0]:
-        to = lax.rem(me + k, T)
-        loads_w[k] = pltpu.make_async_copy(
-            w_hbm.at[:, pl.ds(pl.multiple_of(to * CB, CB), CB)], w_v.at[k], lw.at[k]
-        )
-        loads_w[k].start()
+    pair = me + 1 - 2 * lax.rem(me, 2)
+    across = lax.rem(me + 2, T)
+    if T == 4:
+        blocks = [lax.rem(pair + 2, T), across, pair, me]
+    else:
+        blocks = [lax.rem(me + k, T) for k in far] + [me]
+    loads_w = []
+    for i, to in enumerate(blocks):
+        loads_w.append(pltpu.make_async_copy(
+            w_hbm.at[:, pl.ds(pl.multiple_of(to * CB, CB), CB)], w_v.at[i], lw.at[i]
+        ))
+        loads_w[i].start()
 
     barrier = pltpu.get_barrier_semaphore()
     for k in range(1, T):
@@ -68,13 +73,16 @@
         ).astype(BF16)
     pl.semaphore_wait(barrier, T + O - 2)
 
-    def to_tensor(k, src, dst, ss, rs_):
+    def to_device(i, target, src, dst, ss, rs_):
         c = pltpu.make_async_remote_copy(
-            src_ref=src, dst_ref=dst, send_sem=ss.at[k], recv_sem=rs_.at[k],
-            device_id={"tensor": lax.rem(me + k, T)},
+            src_ref=src, dst_ref=dst, send_sem=ss.at[i], recv_sem=rs_.at[i],
+            device_id={"tensor": target},
         )
         c.start()
         return c
+
+    def to_tensor(k, src, dst, ss, rs_):
+        return to_device(k, lax.rem(me + k, T), src, dst, ss, rs_)
 
     def to_owner(k, target, src, dst, ss, rs_):
         c = pltpu.make_async_remote_copy(
@@ -85,8 +93,9 @@
         return c
 
     sent = []
-    cq = [to_tensor(k, qs.at[lax.rem(me + k, T)], qr.at[me], s_q, r_q) for k in far]
-    sent += cq
+    near = sorted(range(1, T), key=lambda k: min(k, T - k))
+    cq = {k: to_tensor(k, qs.at[lax.rem(me + k, T)], qr.at[me], s_q, r_q) for k in near}
+    sent += cq.values()
     qr[me] = qs[me]
 
     A = abr_ref.shape[1]
@@ -116,36 +125,63 @@
     for o in range(O):
         disp[o, :, KB:] = marks[o * CAP:(o + 1) * CAP, :]
 
-    for c in cq:
-        c.wait_recv()
-    for t in range(T):
-        qf[t * HT * NR:(t + 1) * HT * NR, :] = qr[t].astype(F32)
-
     G = HQ // KVH
-    head_of = lax.broadcasted_iota(jnp.int32, (HQ, KVH * HEAD), 0) // G
-    lane_of = lax.broadcasted_iota(jnp.int32, (HQ, KVH * HEAD), 1) // HEAD
+    for c in loads_k + loads_v:
+        c.wait()
+    KH = max(1, KVH // T)
+    rows_of = KH * G
+    head_of = lax.broadcasted_iota(jnp.int32, (rows_of, KH * HEAD), 0) // G
+    lane_of = lax.broadcasted_iota(jnp.int32, (rows_of, KH * HEAD), 1) // HEAD
     diagonal = head_of == lane_of
-    pos = lax.broadcasted_iota(jnp.int32, (HQ, POS), 1)
-    for r in range(NR):
-        q_r = qf[pl.ds(r, HQ, stride=NR), :]
-        wide = jnp.where(diagonal, jnp.concatenate([q_r] * KVH, axis=1), 0.0).astype(BF16)
-        loads_k[r].wait()
-        scores = lax.dot_general(wide, kv_k[r], NT, preferred_element_type=F32)
-        scores = scores * (1.0 / math.sqrt(HEAD))
-        valid = pos < len_ref[r]
-        scores = jnp.where(valid, scores, -1e30)
+    pos = lax.broadcasted_iota(jnp.int32, (rows_of, POS), 1)
+    valid = [pos < len_ref[r] for r in range(NR)]
+    valid_all = jnp.concatenate(valid, axis=0)
+
+    def attend(first_row, columns):
+        scores = []
+        for r in range(NR):
+            q_r = qf[pl.ds(first_row + r, rows_of, stride=NR), :]
+            wide = jnp.where(diagonal, jnp.concatenate([q_r] * KH, axis=1), 0.0).astype(BF16)
+            scores.append(
+                lax.dot_general(wide, kv_k[r, :, columns], NT, preferred_element_type=F32)
+            )
+        scores = jnp.concatenate(scores, axis=0) * (1.0 / math.sqrt(HEAD))
+        scores = jnp.where(valid_all, scores, -1e30)
         highest = jnp.max(scores, axis=1, keepdims=True)
-        expo = jnp.where(valid, jnp.exp(scores - highest), 0.0)
+        expo = jnp.where(valid_all, jnp.exp(scores - highest), 0.0)
         total = jnp.sum(expo, axis=1, keepdims=True)
-        loads_v[r].wait()
-        mixed = jnp.dot(expo.astype(BF16), kv_v[r], preferred_element_type=F32)
-        mixed = jnp.concatenate(
-            [mixed[g * G:(g + 1) * G, g * HEAD:(g + 1) * HEAD] for g in range(KVH)], axis=0
-        )
-        attf[pl.ds(r, HQ, stride=NR), :] = mixed / total
-    for t in range(T):
-        atts[t] = attf[t * HT * NR:(t + 1) * HT * NR, :].astype(BF16)
-    ca = [to_tensor(k, atts.at[lax.rem(me + k, T)], attr.at[me], s_a, r_a) for k in far]
+        weights = expo.astype(BF16)
+        for r in range(NR):
+            rows = slice(r * rows_of, (r + 1) * rows_of)
+            mixed = jnp.dot(weights[rows], kv_v[r, :, columns], preferred_element_type=F32)
+            mixed = jnp.concatenate(
+                [mixed[g * G:(g + 1) * G, g * HEAD:(g + 1) * HEAD] for g in range(KH)], axis=0
+            )
+            attf[pl.ds(first_row + r, rows_of, stride=NR), :] = mixed / total[rows]
+
+    BR = HT * NR
+    ca = []
+    if KVH % T == 0:
+        for k in [0] + near:
+            d = lax.rem(me + k, T)
+            if k:
+                cq[T - k].wait_recv()
+            first = pl.multiple_of(d * BR, BR)
+            qf[pl.ds(first, BR), :] = qr[d].astype(F32)
+            attend(first, pl.ds(pl.multiple_of(d * KH * HEAD, KH * HEAD), KH * HEAD))
+            atts[d] = attf[pl.ds(first, BR), :].astype(BF16)
+            if k:
+                ca.append(to_tensor(k, atts.at[d], attr.at[me], s_a, r_a))
+    else:
+        for c in cq.values():
+            c.wait_recv()
+        for t in range(T):
+            qf[t * BR:(t + 1) * BR, :] = qr[t].astype(F32)
+        for g in range(KVH):
+            attend(g * G * NR, slice(g * HEAD, (g + 1) * HEAD))
+        for t in range(T):
+            atts[t] = attf[t * BR:(t + 1) * BR, :].astype(BF16)
+        ca = [to_tensor(k, atts.at[lax.rem(me + k, T)], attr.at[me], s_a, r_a) for k in far]
     sent += ca
     attr[me] = atts[me]
 
@@ -176,27 +212,39 @@
     sent += cg
     grecv[mo] = disp[mo]
 
-    def project(k):
-        loads_w[k].wait()
-
-        @pl.loop(0, CB // TN)
+    HB = CB // 2
+
+    def project(i, h, out):
+        if h == 0:
+            loads_w[i].wait()
+
+        @pl.loop(0, HB // TN)
         def _(j):
-            cols = pl.ds(pl.multiple_of(j * TN, TN), TN)
-            part = jnp.dot(xb[...], w_v[k, :, cols], preferred_element_type=F32)
-            if k:
-                ps[k, :, cols] = part.astype(BF16)
-            else:
-                own[:, cols] = part
+            cols = pl.ds(pl.multiple_of(h * HB + j * TN, TN), TN)
+            part = jnp.dot(xb[...], w_v[i, :, cols], preferred_element_type=F32)
+            out[:, cols] = part.astype(out.dtype)
+
+    def half_of(h):
+        return slice(h * HB, (h + 1) * HB)
+
+    def send_sum(i, h, target, slot):
+        return to_device(
+            2 * i + h, target, ps.at[i, :, half_of(h)], pr.at[slot, :, half_of(h)], s_p, r_p
+        )
 
     cp = []
-
-    def project_and_send(k):
-        project(k)
-        cp.append(to_tensor(k, ps.at[k], pr.at[me], s_p, r_p))
-
-    half = max(1, len(far) // 3)
-    for k in far[:half]:
-        project_and_send(k)
+    if T == 4:
+        for h in range(2):
+            project(0, h, ps.at[0])
+            cp.append(send_sum(0, h, pair, 0))
+        for h in range(2):
+            project(1, h, passing)
+    else:
+        half = len(far) // 3
+        for i in range(half):
+            for h in range(2):
+                project(i, h, ps.at[i])
+                cp.append(send_sum(i, h, blocks[i], me))
 
     for c in cg:
         c.wait_recv()
@@ -214,8 +262,20 @@
     cd = [to_tensor(k, ds, dr.at[me], s_d, r_d) for k in far]
     sent += cd
 
-    for k in far[half:]:
-        project_and_send(k)
+    if T == 4:
+        for h in range(2):
+            project(2, h, ps.at[2])
+            cp.append(send_sum(2, h, pair, 2))
+            cp[h].wait_recv()
+            ps[1, :, half_of(h)] = (
+                passing[:, half_of(h)] + pr[0, :, half_of(h)].astype(F32)
+            ).astype(BF16)
+            cp.append(send_sum(1, h, across, 1))
+    else:
+        for i in range(half, len(far)):
+            for h in range(2):
+                project(i, h, ps.at[i])
+                cp.append(send_sum(i, h, blocks[i], me))
     sent += cp
 
     for c in cd:
@@ -236,8 +296,9 @@
     sent += cr
     rr[mo] = rs[mo]
 
-    project(0)
-    for c in cp:
+    for h in range(2):
+        project(T - 1, h, own)
+    for c in cp[2:] if T == 4 else cp:
         c.wait_recv()
     for c in cr:
         c.wait_recv()
@@ -248,8 +309,8 @@
             sel_t[...], rr[:, :, cols].reshape(OC, step), preferred_element_type=F32
         )
         base = own[:, cols]
-        for k in range(1, T):
-            base = base + pr[lax.rem(me + k, T), :, cols].astype(F32)
+        for i in [1, 2] if T == 4 else [lax.rem(me + k, T) for k in range(1, T)]:
+            base = base + pr[i, :, cols].astype(F32)
         out_ref[:, cols] = (base + whole).astype(BF16)
     for c in sent:
         c.wait_send()
@@ -263,7 +324,7 @@
     CAP = 2 * R // O
     OC = O * CAP
     HT = HQ // T
-    TN = min(512, CB)
+    TN = min(512, CB // 2)
     vm = pltpu.VMEM
     dma = pltpu.SemaphoreType.DMA
     scratch = [
@@ -277,10 +338,10 @@
         vm((R, OC), BF16), vm((O, CAP, KB + 128), BF16), vm((O, CAP, KB + 128), BF16),
         vm((OC // 2, 2 * RANK), F32), vm((T, OC // 2, 2 * RANK), F32),
         vm((O, CAP, CB), BF16), vm((O, CAP, CB), BF16),
-        vm((T, R, CB), BF16), vm((T, R, CB), BF16), vm((R, CB), F32),
+        vm((T, R, CB), BF16), vm((T, R, CB), BF16), vm((R, CB), F32), vm((R, CB), F32),
         dma((NR,)), dma((NR,)), dma((T,)), dma(()), dma(()),
         dma((T,)), dma((T,)), dma((T,)), dma((T,)), dma((O,)), dma((O,)),
-        dma((T,)), dma((T,)), dma((O,)), dma((O,)), dma((T,)), dma((T,)),
+        dma((T,)), dma((T,)), dma((O,)), dma((O,)), dma((2 * T,)), dma((2 * T,)),
     ]
     any_spec = pl.BlockSpec(memory_space=pl.ANY)
     vmem_spec = pl.BlockSpec(memory_space=pltpu.VMEM)

time: 38.9 us -> 36.8 us (0.946)
  Pallas kernels: 37.1 us -> 35.1 us
    pallas_call x1, Pallas kernels: 37.1 us -> 35.1 us  [local(): pl.pallas_call(functools.partial(kernel, T, O, CAP, TN), out_shape=jax.Sh...]
where the time goes in v2:
time: 36.8 us; the launch traced here: 36.7 us
  Pallas kernels  35.1 us (95%)
  local copies, waits for them, and re-layouts  1.57 us (4%)
    pallas_call x1, Pallas kernels, local(): pl.pallas_call(functools.partial(kernel, T, O, CAP, TN), out_shape=jax.Sh...  35.1 us
    unnamed x1, local copies, waits for them, and re-layouts  1.57 us

profile of v2, /device:TPU:0, one launch (start us, length us, event | category | flops | bytes accessed | tf_op | source)
XLA Modules:
  0.0 36.7 jit_solution(5490056936637562982)
XLA Ops:
  0.0 35.1 %attend_project_adapt.1 = bf16[32,2048]{1,0:T(8,128)(2,1)} custom-call(bf16[32,2048]{1,0:T(8,128)(2,1)} %q_ref.1, s32[8]{0:T(128)} %len_ref.1, s32[1,32]{1,0:T(1,128)} %bitcast.4, s32[1,32]{1,0:T(1,128)} %bitcast.5, bf16[8,192,1024]{2,1,0:T(8,128)(2,1)} %k_hbm.1, bf16[8,192,1024]{2,1,0:T(8,128)(2,1)} %v_hbm.1, bf16[2048,8192]{1,0:T(8,128)(2,1)} %w_hbm.1, ...), custom_call_target="tpu_custom_call" | custom-call | tf_op jit(solution)/shard_map/attend_project_adapt/pallas_call | solution.py:349
  35.1 1.6 %copy.11 = bf16[32,2048]{1,0:T(8,128)(2,1)} copy(bf16[32,2048]{1,0:T(8,128)(2,1)} %attend_project_adapt.1) | data formatting | bytes 262144

commit v3 on v2

--- a/solution.py
+++ b/solution.py
@@ -58,7 +58,13 @@
         loads_w.append(pltpu.make_async_copy(
             w_hbm.at[:, pl.ds(pl.multiple_of(to * CB, CB), CB)], w_v.at[i], lw.at[i]
         ))
-        loads_w[i].start()
+
+    def fetch(first, last):
+        for i in range(first, min(last, T)):
+            loads_w[i].start()
+
+
+    fetch(0, 2)
 
     barrier = pltpu.get_barrier_semaphore()
     for k in range(1, T):
@@ -162,6 +168,7 @@
     BR = HT * NR
     ca = []
     if KVH % T == 0:
+        started = 2
         for k in [0] + near:
             d = lax.rem(me + k, T)
             if k:
@@ -172,7 +179,11 @@
             atts[d] = attf[pl.ds(first, BR), :].astype(BF16)
             if k:
                 ca.append(to_tensor(k, atts.at[d], attr.at[me], s_a, r_a))
+            fetch(started, started + 1)
+            started += 1
+        fetch(started, T)
     else:
+        fetch(2, T)
         for c in cq.values():
             c.wait_recv()
         for t in range(T):

time: 36.8 us -> 32.4 us (0.88)
  Pallas kernels: 35.1 us -> 30.6 us
    pallas_call x1, Pallas kernels: 35.1 us -> 30.6 us  [local(): pl.pallas_call(functools.partial(kernel, T, O, CAP, TN), out_shape=jax.Sh...]
where the time goes in v3:
time: 32.4 us; the launch traced here: 32.2 us
  Pallas kernels  30.6 us (94%)
  local copies, waits for them, and re-layouts  1.57 us (5%)
    pallas_call x1, Pallas kernels, local(): pl.pallas_call(functools.partial(kernel, T, O, CAP, TN), out_shape=jax.Sh...  30.6 us
    unnamed x1, local copies, waits for them, and re-layouts  1.57 us

profile of v3, /device:TPU:0, one launch (start us, length us, event | category | flops | bytes accessed | tf_op | source)
XLA Modules:
  0.0 32.2 jit_solution(10766339670353708417)
XLA Ops:
  0.0 30.6 %attend_project_adapt.1 = bf16[32,2048]{1,0:T(8,128)(2,1)} custom-call(bf16[32,2048]{1,0:T(8,128)(2,1)} %q_ref.1, s32[8]{0:T(128)} %len_ref.1, s32[1,32]{1,0:T(1,128)} %bitcast.4, s32[1,32]{1,0:T(1,128)} %bitcast.5, bf16[8,192,1024]{2,1,0:T(8,128)(2,1)} %k_hbm.1, bf16[8,192,1024]{2,1,0:T(8,128)(2,1)} %v_hbm.1, bf16[2048,8192]{1,0:T(8,128)(2,1)} %w_hbm.1, ...), custom_call_target="tpu_custom_call" | custom-call | tf_op jit(solution)/shard_map/attend_project_adapt/pallas_call | solution.py:360
  30.7 1.6 %copy.11 = bf16[32,2048]{1,0:T(8,128)(2,1)} copy(bf16[32,2048]{1,0:T(8,128)(2,1)} %attend_project_adapt.1) | data formatting | bytes 262144

commit v4 on v3

--- a/solution.py
+++ b/solution.py
@@ -275,13 +275,14 @@
 
     if T == 4:
         for h in range(2):
-            project(2, h, ps.at[2])
-            cp.append(send_sum(2, h, pair, 2))
             cp[h].wait_recv()
             ps[1, :, half_of(h)] = (
                 passing[:, half_of(h)] + pr[0, :, half_of(h)].astype(F32)
             ).astype(BF16)
             cp.append(send_sum(1, h, across, 1))
+        for h in range(2):
+            project(2, h, ps.at[2])
+            cp.append(send_sum(2, h, pair, 2))
     else:
         for i in range(half, len(far)):
             for h in range(2):

time: 32.4 us -> 32.3 us (level)
  no operation moved by 1% of the time
where the time goes in v4:
time: 32.3 us; the launch traced here: 32.2 us
  Pallas kernels  30.6 us (95%)
  local copies, waits for them, and re-layouts  1.57 us (5%)
    pallas_call x1, Pallas kernels, local(): pl.pallas_call(functools.partial(kernel, T, O, CAP, TN), out_shape=jax.Sh...  30.6 us
    unnamed x1, local copies, waits for them, and re-layouts  1.57 us

profile of v4, /device:TPU:0, one launch (start us, length us, event | category | flops | bytes accessed | tf_op | source)
XLA Modules:
  0.0 32.2 jit_solution(2883212191140827891)
XLA Ops:
  0.0 30.6 %attend_project_adapt.1 = bf16[32,2048]{1,0:T(8,128)(2,1)} custom-call(bf16[32,2048]{1,0:T(8,128)(2,1)} %q_ref.1, s32[8]{0:T(128)} %len_ref.1, s32[1,32]{1,0:T(1,128)} %bitcast.4, s32[1,32]{1,0:T(1,128)} %bitcast.5, bf16[8,192,1024]{2,1,0:T(8,128)(2,1)} %k_hbm.1, bf16[8,192,1024]{2,1,0:T(8,128)(2,1)} %v_hbm.1, bf16[2048,8192]{1,0:T(8,128)(2,1)} %w_hbm.1, ...), custom_call_target="tpu_custom_call" | custom-call | tf_op jit(solution)/shard_map/attend_project_adapt/pallas_call | solution.py:361
  30.6 1.6 %copy.11 = bf16[32,2048]{1,0:T(8,128)(2,1)} copy(bf16[32,2048]{1,0:T(8,128)(2,1)} %attend_project_adapt.1) | data formatting | bytes 262144
